TPU v7x, 512 devices: a whole 4x4x16 slice. The times are simulated.
512 devices in a mesh: dp: 128 (over z, y_lo, x), head: 4 (over y_hi, core).
Axes of the slice: x: 4, y: 4 (y_hi: 2, y_lo: 2; y = y_hi * 2 + y_lo), z: 16, core: 2. Of those that a mesh axis runs over, the one named last changes fastest.
Arguments:
- queries: bfloat16 [128, 24, 512, 128], P('dp', None, 'head'), may hold values from -6.5 to 6.5
- key_rows: bfloat16 [128, 24, 512, 128], P('dp', None, 'head'), may hold values from -6.5 to 6.5
- value_rows: bfloat16 [128, 24, 512, 128], P('dp', None, 'head'), may hold values from -6 to 6
- upstream: bfloat16 [128, 24, 512, 128], P('dp', None, 'head'), may hold values from -24 to 24
- activations: bfloat16 [128, 512, 6144], P('dp', None, 'head'), may hold values from -14 to 14
Outputs:
- act_inv: bfloat16 [6144, 128], P(('head', 'dp'))
- grad_inv: bfloat16 [9216, 128], P(('head', 'dp'))
All inputs are finite; a program needn't handle non-finite values.
Results may differ from a plain program's by a relative error of at most 0.0031.
The roundings to bfloat16 on the way count: a program that leaves them out, or rounds other values in their place, can miss the bound.
Values may be sent and summed in bfloat16 or wider, within the bound.
A program may use at most 64 MiB of HBM per device.

v0:
```python
import math

import jax
import jax.numpy as jnp
from jax import lax
from jax.sharding import PartitionSpec as P

DAMPING = 0.1


def attend_back(queries, key_rows, value_rows, upstream):
    length, head_size = queries.shape
    block_rows = min(512, length)
    score_scale = 1.0 / math.sqrt(head_size)

    def one_block(partial_value, turn_index):
        key_grad, value_grad = partial_value
        scores = jnp.dot(queries, key_rows.T, preferred_element_type=jnp.float32) * score_scale
        row_top = jnp.max(scores, axis=1, keepdims=True)
        weights = jnp.exp(scores - row_top)
        probs_full = weights / jnp.sum(weights, axis=1, keepdims=True)
        probs_half = probs_full.astype(jnp.bfloat16)
        output = jnp.dot(probs_half, value_rows, preferred_element_type=jnp.float32)
        row_delta = jnp.sum(upstream.astype(jnp.float32) * output, axis=1, keepdims=True)
        probs_grad = jnp.dot(upstream, value_rows.T, preferred_element_type=jnp.float32)
        score_grad = (probs_full * (probs_grad - row_delta)).astype(jnp.bfloat16)
        query_grad = (
            jnp.dot(score_grad, key_rows, preferred_element_type=jnp.float32) * score_scale
        ).astype(jnp.bfloat16)
        key_grad = key_grad + jnp.dot(score_grad.T, queries, preferred_element_type=jnp.float32)
        value_grad = value_grad + jnp.dot(
            probs_half.T, upstream, preferred_element_type=jnp.float32
        )
        return ((key_grad, value_grad), query_grad)

    empty_grad = jnp.zeros((length, head_size), jnp.float32)
    partial_value, query_grad = lax.scan(
        one_block, (empty_grad, empty_grad), jnp.arange(length // block_rows)
    )
    query_grad = query_grad.reshape(length, head_size)
    key_grad = (partial_value[0] * score_scale).astype(jnp.bfloat16)
    value_grad = partial_value[1].astype(jnp.bfloat16)
    return (query_grad, key_grad, value_grad)


def damped_inverse(gram_blocks):
    head_size = gram_blocks.shape[-1]
    trace_value = jnp.trace(gram_blocks, axis1=1, axis2=2)
    identity = jnp.eye(head_size, dtype=jnp.float32)
    damped = gram_blocks / (trace_value[:, None, None] / head_size + 1e-06) + DAMPING * identity
    lower_factor = jnp.linalg.cholesky(damped)
    identities = jnp.broadcast_to(identity, damped.shape)
    lower_inverse = lax.linalg.triangular_solve(
        lower_factor, identities, left_side=True, lower=True
    )
    return jnp.einsum("nkc,nkd->ncd", lower_inverse, lower_inverse, precision=lax.Precision.HIGHEST)


def my_rows(blocks):
    flat_rows = blocks.reshape(blocks.shape[0] * blocks.shape[1], blocks.shape[2])
    row_count = flat_rows.shape[0] // lax.axis_size("dp")
    return lax.dynamic_slice_in_dim(flat_rows, lax.axis_index("dp") * row_count, row_count, 0)


def per_pair(pair_items):
    return attend_back(pair_items[0], pair_items[1], pair_items[2], pair_items[3])


def per_device(queries, key_rows, value_rows, upstream, activations):
    images, heads_all, rows_here, head_size = queries.shape
    blocks_here = activations.shape[2] // head_size
    acts_flat = activations.reshape(images * activations.shape[1], blocks_here, head_size)
    act_local = jnp.einsum("tbc,tbd->bcd", acts_flat, acts_flat, preferred_element_type=jnp.float32)
    act_gram = lax.psum(act_local, "dp")
    owned_rows = (
        lax.all_to_all(queries, "head", split_axis=1, concat_axis=2, tiled=True),
        lax.all_to_all(key_rows, "head", split_axis=1, concat_axis=2, tiled=True),
        lax.all_to_all(value_rows, "head", split_axis=1, concat_axis=2, tiled=True),
        lax.all_to_all(upstream, "head", split_axis=1, concat_axis=2, tiled=True),
    )
    images_own, heads_own, length, unused = owned_rows[0].shape
    pairs = images_own * heads_own
    flat_items = tuple((item.reshape(pairs, length, head_size) for item in owned_rows))
    query_grad, key_grad, value_grad = lax.map(per_pair, flat_items)
    grad_rows = jnp.stack([query_grad, key_grad, value_grad], 0).reshape(
        3, images_own, heads_own, length, head_size
    )
    grad_local = jnp.einsum(
        "pihlc,pihld->hpcd", grad_rows, grad_rows, preferred_element_type=jnp.float32
    )
    grad_gram = lax.psum(grad_local, "dp")
    all_grams = jnp.concatenate(
        [act_gram, grad_gram.reshape(heads_own * 3, head_size, head_size)], 0
    )
    inverses = damped_inverse(all_grams).astype(jnp.bfloat16)
    act_inv = my_rows(inverses[:blocks_here])
    grad_inv = my_rows(inverses[blocks_here:])
    return (act_inv, grad_inv)


def solution(mesh):
    in_specs = (
        P("dp", None, "head", None),
        P("dp", None, "head", None),
        P("dp", None, "head", None),
        P("dp", None, "head", None),
        P("dp", None, "head"),
    )
    out_specs = (P(("head", "dp"), None), P(("head", "dp"), None))
    return jax.shard_map(
        per_device, mesh=mesh, in_specs=in_specs, out_specs=out_specs, check_vma=False
    )
```

profile of v0, /device:TPU:8, one launch (start us, length us, event | category | flops | bytes accessed | tf_op | source)
XLA Modules:
  0.0 1989.7 jit_solution(1240151500568790402)
XLA Ops:
  7.2 17.6 all_to_all.60
  24.7 16.3 all_to_all.61
  41.0 15.6 all_to_all.62
  56.6 3.5 all-to-all-start.3
  60.1 1.7 copy.43
  61.9 1.5 fusion.50
  63.3 1.6 copy.50
  66.3 6.9 all-to-all-done.3
  74.1 38.7 %while.14 = (s32[]{:T(128)}, bf16[6,512,128]{2,1,0:T(8,128)(2,1)}, bf16[6,512,128]{2,1,0:T(8,128)(2,1)}, bf16[6,512,128]{2,1,0:T(8,128)(2,1)}, bf16[6,512,128]{2...) while((s32[]{:T(128)}, bf16[6,512,128]{2,1,0:T(8,128)(2,1)}, ...), condition=%wide.region_5.6_spmd, body=%wide.region_1.5_spmd.sunk | while | flops 406321664 | bytes 12083321 | solution.py:84
  75.3 1.2 fusion.90
  76.5 1.2 fusion.91
  81.7 1.2 fusion.90
  82.9 1.2 fusion.91
  88.2 1.2 fusion.90
  89.3 1.2 fusion.91
  94.6 1.2 fusion.90
  95.8 1.2 fusion.91
  101.1 1.2 fusion.90
  102.2 1.2 fusion.91
  107.5 1.2 fusion.90
  108.7 1.2 fusion.91
  112.8 4.3 fusion.36
  117.3 1198.2 %all-reduce.3.cloned.1.call-done = (f32[12,128,128]{2,1,0:T(8,128)}, f32[18,128,128]{2,1,0:T(8,128)}) async-done(((f32[12,128,128]{2,1,0:T(8,128)}, f32[18,128,128]{2,1,0:T(8,128)}), (f32[12,128,128]{2,1,0:T(8,128)}, f32[18,128,128]{2,1,0:T(8,128)})) %all-reduce.3.cloned.1.call-update) | async-done | bytes 1966096 | tf_op jit(solution)/shard_map/psum | solution.py:74
  1315.4 1.3 constant_dynamic-update-slice_fusion.1
  1317.4 1.6 divide_add_fusion
  1318.9 2.8 copy.54
  1321.8 3.3 fusion.44
  1325.0 352.3 %custom-call.7 = f32[30,128,128]{2,1,0:T(8,128)S(1)} custom-call(f32[30,128,128]{2,1,0:T(8,128)} %fusion.44), custom_call_target="Cholesky" | custom-call | tf_op jit(solution)/shard_map/jit(cholesky)/cholesky | solution.py:51
  1677.7 1.6 select_bitcast_fusion
  1679.2 295.6 %custom-call.8 = f32[30,1,128,128]{2,3,1,0:T(8,128)S(1)} custom-call(f32[30,1,128,128]{3,2,1,0:T(8,128)} %select_bitcast_fusion), custom_call_target="InvertDiagBlocksLowerTriangular" | custom-call | tf_op jit(solution)/shard_map/triangular_solve | solution.py:53
  1974.8 3.2 fusion.42
  1978.1 3.5 convolution_convert_fusion.1
  (78 shorter events, 28.7 us)
Async XLA Ops:
  7.2 17.6 copy-start.3
  7.2 33.8 %copy-start.4 = (bf16[1,24,128,128]{3,2,1,0:T(8,128)(2,1)S(1)}, bf16[1,24,128,128]{3,2,1,0:T(8,128)(2,1)}, u32[]{:S(2)}) copy-start(bf16[1,24,128,128]{3,2,1,0:T(8,128)(2,1)} %param.8) | copy-start | bytes 2359300
  56.6 16.6 all-to-all-start.3
  60.1 1255.4 %all-reduce.3.cloned.1.call-start = ((), (), s32[]{:S(2)}) async-start(), calls=%async_computation.4 | async-start | bytes 3932160 | tf_op jit(solution)/shard_map/psum | solution.py:74
  63.3 2.8 copy-start
  74.2 1.1 copy-start.1
  80.6 1.1 copy-start.1
  87.0 1.1 copy-start.1
  93.5 1.1 copy-start.1
  99.9 1.1 copy-start.1
  106.4 1.1 copy-start.1
  1315.4 1.5 copy-start.2
Sparse Core Ops, SparseCore 0:
  117.3 1198.0 all-reduce.2
where the time goes:
time: 1990 us
  waiting for transfers between devices  1210 us (61%)
  other arithmetic  657 us (33%)
  blocking collectives  49.4 us (2%)
  matrix products  46.1 us (2%)
    psum x1, waiting for transfers between devices, per_device(): act_gram = lax.psum(act_local, 'dp')  1200 us
    another operation x4, other arithmetic, damped_inverse(): lower_factor = jnp.linalg.cholesky(damped)  353 us
    another operation x3, other arithmetic, damped_inverse(): lax.linalg.triangular_solve(lower_factor, identities, left_side=True, low...  297 us
  transfers between devices with their start and end apart: 2, of which 2 were waited for; matrix products, arithmetic and copies ran while one was open for 0% of the time, Pallas kernels for 0%

commit v1 on v0

v1 whole, which is shorter than its diff:
```python
import math

import jax
import jax.numpy as jnp
from jax import lax
from jax.experimental import pallas as pl
from jax.experimental.pallas import tpu as pltpu
from jax.sharding import PartitionSpec as P

DAMPING = 0.1
XN, YN, ZN = 4, 2, 16
GROUP = XN * YN * ZN
HD = 128
LEN = 512
OWN = 6
QUERIES = 256
PANEL = 16
SLOTS = 8
SCALE = 1.0 / math.sqrt(HD)
LOG2E = 1.4426950408889634
MESH = pl.DeviceIdType.MESH
F32 = jnp.float32
BF16 = jnp.bfloat16


def dot(a, b, a_dim, b_dim):
    return lax.dot_general(a, b, (((a_dim,), (b_dim,)), ((), ())), preferred_element_type=F32)


def head_grams(rows):
    q, k, v, u = rows[0], rows[1], rows[2], rows[3]
    blocks = range(0, LEN, QUERIES)
    probs, probs_half = [], []
    for i in blocks:
        scores = dot(k, q[i : i + QUERIES], 1, 1)
        top = jnp.max(scores, axis=0, keepdims=True)
        weights = jnp.exp2((scores - top) * (SCALE * LOG2E))
        probs.append(weights * (1.0 / jnp.sum(weights, axis=0, keepdims=True)))
        probs_half.append(probs[-1].astype(BF16))
    probs_grad = [dot(v, u[i : i + QUERIES], 1, 1) for i in blocks]
    score_grad = []
    for full, half, grad in zip(probs, probs_half, probs_grad):
        row_delta = jnp.sum(half.astype(F32) * grad, axis=0, keepdims=True)
        score_grad.append((full * (grad - row_delta)).astype(BF16))
    value_grad = sum(dot(p, u[i : i + QUERIES], 1, 0) for p, i in zip(probs_half, blocks))
    value_grad = value_grad.astype(BF16)
    yield 2, dot(value_grad, value_grad, 0, 0)
    key_grad = sum(dot(g, q[i : i + QUERIES], 1, 0) for g, i in zip(score_grad, blocks))
    key_grad = (key_grad * SCALE).astype(BF16)
    yield 1, dot(key_grad, key_grad, 0, 0)
    query_grad = [(dot(k, g, 0, 0) * SCALE).astype(BF16) for g in score_grad]
    yield 0, sum(dot(g, g, 1, 1) for g in query_grad)


def invert_in_place(a_ref):
    lane = lax.broadcasted_iota(jnp.int32, (8, HD), 1)
    row = lax.broadcasted_iota(jnp.int32, (PANEL, HD), 0).reshape(PANEL // 8, 8, HD)
    done = lax.broadcasted_iota(jnp.int32, (HD, HD), 1) < PANEL

    def panel_step(panel, carry):
        rows = pl.ds(pl.multiple_of(panel * PANEL, PANEL), PANEL)
        full = a_ref[...]
        pivots = a_ref[rows, :].reshape(PANEL // 8, 8, HD)
        for s in range(0, PANEL, 2):
            g, r = s // 8, s % 8
            first, second = lane == s, lane == s + 1
            both = first | second

            def spread(i, j):
                return jnp.broadcast_to(
                    pivots[g, r + i : r + i + 1, s + j : s + j + 1], (8, HD)
                )

            a, b, d = spread(0, 0), spread(0, 1), spread(1, 1)
            inv = 1.0 / (a * d - b * b)
            row_a = jnp.broadcast_to(pivots[g, r : r + 1, :], (8, HD))
            row_b = jnp.broadcast_to(pivots[g, r + 1 : r + 2, :], (8, HD))
            row_a = jnp.where(first, 1.0, jnp.where(second, 0.0, row_a))
            row_b = jnp.where(first, 0.0, jnp.where(second, 1.0, row_b))
            new_a = (d * row_a - b * row_b) * inv
            new_b = (a * row_b - b * row_a) * inv
            others = (
                jnp.where(both[None], 0.0, pivots)
                - pivots[:, :, s : s + 1] * new_a[None]
                - pivots[:, :, s + 1 : s + 2] * new_b[None]
            )
            pivots = jnp.where(
                row == s, new_a[None], jnp.where(row == s + 1, new_b[None], others)
            )
        pivots = pivots.reshape(PANEL, HD)
        a_ref[...] = jnp.where(done, 0.0, full) - lax.dot_general(
            full[:, :PANEL], pivots, (((1,), (0,)), ((), ())),
            precision=lax.Precision.HIGHEST, preferred_element_type=F32,
        )
        a_ref[rows, :] = pivots
        a_ref[...] = pltpu.roll(a_ref[...], HD - PANEL, 1)
        return carry

    lax.fori_loop(0, HD // PANEL, panel_step, 0)


def whole_kernel(
    q_hbm, k_hbm, v_hbm, u_hbm, acts_hbm, act_out, grad_out,
    acts, buf, gram, x_in, x_sum, z_in, z_sum, parts, block, act_win, grad_win,
    acts_sem, buf_recv, core_send, far_send,
    xa_send, xg_send, x_recv, z_send, z_recv, g_send, g_recv, w_send, act_recv, grad_recv,
):
    tensors = (q_hbm, k_hbm, v_hbm, u_hbm)
    dp = lax.axis_index("dp")
    head = lax.axis_index("head")
    x = dp % XN
    y = (dp // XN) % YN
    z = dp // (XN * YN)
    core = head % 2
    half = head // 2

    def place(z_, y_, x_, head_):
        return (z_ * (XN * YN) + y_ * XN + x_, head_)

    def copy(src, dst, send, recv, device):
        return pltpu.make_async_remote_copy(
            src_ref=src, dst_ref=dst, send_sem=send, recv_sem=recv,
            device_id=device, device_id_type=MESH,
        )

    def wait_bytes(ref, sem):
        pltpu.make_async_copy(ref, ref, sem).wait()

    def rows_of(source):
        return pl.ds(pl.multiple_of(source * HD, HD), HD)

    def start_head(t):
        for i in range(4):
            for far in range(2):
                to = (1 - half) * 2 + far
                copy(
                    tensors[i].at[0, to * OWN + t], buf.at[t, i, rows_of(head), :],
                    far_send.at[t], buf_recv.at[t], place(z, y, x, to),
                ).start()
        other = half * 2 + 1 - core
        for i in range(4):
            copy(
                tensors[i].at[0, other * OWN + t], buf.at[t, i, rows_of(head), :],
                core_send.at[t], buf_recv.at[t], place(z, y, x, other),
            ).start()
            pltpu.make_async_copy(
                tensors[i].at[0, head * OWN + t], buf.at[t, i, rows_of(head), :],
                buf_recv.at[t],
            ).start()

    stage_slots = ((0, 3), (3, 3), (6, 1), (7, 1))

    def act_copy(r):
        to = (x + r) % XN
        return copy(
            gram.at[to, pl.ds(0, 3)], x_in.at[3 - r, pl.ds(0, 3)],
            xa_send.at[r - 1], x_recv.at[0], place(z, y, to, head),
        )

    def grad_place(t, p):
        n = 3 * t + p
        early = t < 4
        owner = jnp.where(early, n % XN, p)
        slot = jnp.where(early, 3 + n // XN, t + 2)
        stage = jnp.where(early, 1, t - 2)
        return n, owner, slot, stage

    def grad_copy(t, p):
        n, owner, slot, stage = grad_place(t, p)
        r = (x - owner + XN) % XN
        return owner, copy(
            gram.at[owner, slot], x_in.at[jnp.maximum(r - 1, 0), slot],
            xg_send.at[n], x_recv.at[stage], place(z, y, owner, head),
        )

    def compute_head(t):
        wait_bytes(buf.at[t], buf_recv.at[t])
        for p, block_gram in head_grams([buf[t, i] for i in range(4)]):
            unused, owner, slot, unused = grad_place(t, p)
            gram[owner, slot] = block_gram
            owner, send = grad_copy(t, p)
            pl.when(owner != x)(send.start)

    def z_piece(stage, to):
        first, count = stage_slots[stage]
        src = x_sum.at[pl.ds(first, count), pl.ds(pl.multiple_of(to * 8, 8), 8), :]
        return src, z_in.at[z, pl.ds(first, count)]

    def sum_x(stage):
        first, count = stage_slots[stage]
        slots = pl.ds(first, count)
        wait_bytes(x_in.at[:, slots], x_recv.at[stage])
        for s in range(first, first + count):
            x_sum[s] = (gram[x, s] + x_in[0, s]) + (x_in[1, s] + x_in[2, s])

        def send(to, carry):
            src, dst = z_piece(stage, to)

            @pl.when(to != z)
            def _():
                copy(
                    src, dst, z_send.at[stage], z_recv.at[stage], place(to, y, x, head)
                ).start()

            @pl.when(to == z)
            def _():
                pltpu.make_async_copy(src, dst, z_recv.at[stage]).start()

            return carry

        lax.fori_loop(0, ZN, send, 0)

    def sum_z(stage):
        first, count = stage_slots[stage]
        wait_bytes(z_in.at[:, pl.ds(first, count)], z_recv.at[stage])
        for s in range(first, first + count):
            z_sum[s] = jnp.sum(z_in[:, s], axis=0)
            dst = parts.at[y, pl.ds(pl.multiple_of(z * 8, 8), 8), :]
            mine = (z == 2 * s) & (y == 0)

            @pl.when(jnp.logical_not(mine))
            def _():
                copy(
                    z_sum.at[s], dst, g_send.at[s], g_recv, place(2 * s, 0, x, head)
                ).start()

            @pl.when(mine)
            def _():
                pltpu.make_async_copy(z_sum.at[s], dst, g_recv).start()

    late = x < 3

    def drain():
        def sent(t, carry):
            wait_bytes(buf.at[t, :, pl.ds(0, 2 * HD), :], far_send.at[t])
            wait_bytes(buf.at[t, :, pl.ds(0, HD), :], core_send.at[t])
            for p in range(3):
                owner, send = grad_copy(t, p)
                pl.when(owner != x)(send.wait_send)
            return carry

        lax.fori_loop(0, OWN, sent, 0)
        for r in (1, 3, 2):
            act_copy(r).wait_send()
        for stage, (first, count) in enumerate(stage_slots):
            def drain_stage():
                wait_bytes(z_in.at[pl.ds(0, ZN - 1), pl.ds(first, count)], z_send.at[stage])
                for s in range(first, first + count):
                    @pl.when(jnp.logical_not((z == 2 * s) & (y == 0)))
                    def _():
                        wait_bytes(z_sum.at[s], g_send.at[s])

            drain_stage() if stage < 2 else pl.when(late)(drain_stage)

    load = pltpu.make_async_copy(acts_hbm.at[0], acts, acts_sem)
    load.start()

    barrier = pltpu.get_barrier_semaphore()
    for r in range(1, 4):
        pl.semaphore_signal(
            barrier, inc=1, device_id=(dp, (head + r) % 4), device_id_type=MESH
        )

    def greet(r, carry):
        pl.semaphore_signal(
            barrier, inc=1, device_id=((dp + r) % GROUP, head), device_id_type=MESH
        )
        return carry

    lax.fori_loop(1, GROUP, greet, 0)
    pl.semaphore_wait(barrier, GROUP - 1 + 3)

    def start(t, carry):
        start_head(t)
        return carry

    lax.fori_loop(0, OWN, start, 0)
    load.wait()

    def act_gram(b, carry):
        item = acts[:, pl.ds(pl.multiple_of(b * HD, HD), HD)]
        gram[b // 3, b % 3] = dot(item, item, 0, 0)
        return carry

    lax.fori_loop(0, 12, act_gram, 0)
    for r in (2, 1, 3):
        act_copy(r).start()

    def step(t, carry):
        @pl.when(t == 3)
        def _():
            sum_x(0)

        @pl.when(t == 5)
        def _():
            sum_z(0)

        compute_head(t - 1)

        @pl.when(t == 5)
        def _():
            sum_x(1)

        return carry

    lax.fori_loop(1, OWN + 1, step, 0)
    pl.when(late)(lambda: sum_x(2))
    sum_z(1)
    pl.when(late)(lambda: sum_x(3))
    pl.when(late)(lambda: sum_z(2))
    pl.when(late)(lambda: sum_z(3))

    drain()
    slot = z // 2
    act_index = x * 3 + slot
    act_first = (act_index * 32) // 3
    grad_index = jnp.where(slot < 6, (slot - 3) * 4 + x, 12 + (slot - 6) * 3 + x)
    grad_first = (jnp.maximum(grad_index, 0) * 64) // 9
    inverter = (z % 2 == 0) & (y == 0) & ((slot < 6) | late)

    @pl.when(inverter)
    def _():
        wait_bytes(parts, g_recv)
        eye = lax.broadcasted_iota(jnp.int32, (HD, HD), 0) == lax.broadcasted_iota(
            jnp.int32, (HD, HD), 1
        )
        total = parts[0] + parts[1]
        trace = jnp.sum(jnp.where(eye, total, 0.0), axis=(0, 1), keepdims=True)
        block[...] = total / (trace / HD + 1e-06) + jnp.where(eye, DAMPING, 0.0)
        invert_in_place(block)


    def hand_out(block_index, first_to, count, pieces, window, recv, start):
        def one(i, carry):
            to = first_to + i
            for p in range(pieces):
                if pieces == 2:
                    piece = (3 * to) // 2 + p - 16 * block_index
                else:
                    piece = (9 * to) // 4 + p - 16 * block_index
                use = (piece >= 0) & (piece < 16)
                src = block.at[pl.ds(pl.multiple_of(piece * 8, 8), 8), :]
                dst = window.at[pl.ds(8 * p, 8), :]

                @pl.when(use & (to != dp))
                def _():
                    c = copy(src, dst, w_send.at[p, i], recv.at[p], (to, head))
                    c.start() if start else c.wait_send()

                if start:
                    @pl.when(use & (to == dp))
                    def _():
                        pltpu.make_async_copy(src, dst, recv.at[p]).start()

            return carry

        lax.fori_loop(0, count, one, 0)

    def each_piece(start):
        @pl.when(inverter & (slot < 3))
        def _():
            hand_out(act_index, act_first, 12, 2, act_win, act_recv, start)

        @pl.when(inverter & (slot >= 3))
        def _():
            hand_out(grad_index, grad_first, 9, 3, grad_win, grad_recv, start)

    each_piece(True)
    for s in range(2):
        wait_bytes(act_win.at[pl.ds(8 * s, 8), :], act_recv.at[s])
    for s in range(3):
        wait_bytes(grad_win.at[pl.ds(8 * s, 8), :], grad_recv.at[s])
    rows = act_win[...]
    act_out[...] = jnp.where(dp % 2 == 0, rows[0:12], rows[4:16]).astype(BF16)
    rows = grad_win[...]
    odd = dp % 4
    grad_out[...] = jnp.where(
        odd < 2,
        jnp.where(odd == 0, rows[0:18], rows[2:20]),
        jnp.where(odd == 2, rows[4:22], rows[6:24]),
    ).astype(BF16)

    each_piece(False)


def per_device(queries, key_rows, value_rows, upstream, activations):
    vmem = pl.BlockSpec(memory_space=pltpu.VMEM)
    hbm = pl.BlockSpec(memory_space=pltpu.HBM)
    dma = pltpu.SemaphoreType.DMA
    return pl.pallas_call(
        whole_kernel,
        out_shape=(
            jax.ShapeDtypeStruct((12, HD), BF16),
            jax.ShapeDtypeStruct((18, HD), BF16),
        ),
        in_specs=[hbm] * 5,
        out_specs=(vmem, vmem),
        scratch_shapes=[
            pltpu.VMEM((LEN, 12 * HD), BF16),
            pltpu.VMEM((OWN, 4, LEN, HD), BF16),
            pltpu.VMEM((XN, SLOTS, HD, HD), F32),
            pltpu.VMEM((XN - 1, SLOTS, HD, HD), F32),
            pltpu.VMEM((SLOTS, HD, HD), F32),
            pltpu.VMEM((ZN, SLOTS, 8, HD), F32),
            pltpu.VMEM((SLOTS, 8, HD), F32),
            pltpu.VMEM((YN, HD, HD), F32),
            pltpu.VMEM((HD, HD), F32),
            pltpu.VMEM((16, HD), F32),
            pltpu.VMEM((24, HD), F32),
            dma, dma((OWN,)), dma((OWN,)), dma((OWN,)),
            dma((3,)), dma((18,)), dma((4,)), dma((4,)), dma((4,)), dma((SLOTS,)), dma,
            dma((3, 12)), dma((2,)), dma((3,)),
        ],
        compiler_params=pltpu.CompilerParams(
            collective_id=0, has_side_effects=True, vmem_limit_bytes=62 * 1024 * 1024
        ),
        cost_estimate=pl.CostEstimate(
            flops=4_000_000_000, bytes_accessed=5_000_000, transcendentals=1_600_000
        ),
    )(queries, key_rows, value_rows, upstream, activations)


def solution(mesh):
    in_specs = (
        P("dp", None, "head", None),
        P("dp", None, "head", None),
        P("dp", None, "head", None),
        P("dp", None, "head", None),
        P("dp", None, "head"),
    )
    out_specs = (P(("head", "dp"), None), P(("head", "dp"), None))
    return jax.shard_map(
        per_device, mesh=mesh, in_specs=in_specs, out_specs=out_specs, check_vma=False
    )
```

time: 1990 us -> 98.4 us (0.05)
  the two profiles are of different devices: /device:TPU:8 before, /device:TPU:14 now
where the time goes in v1:
time: 98.4 us; the launch traced here: 98.2 us
  Pallas kernels  95 us (97%)
  local copies, waits for them, and re-layouts  2.55 us (3%)
    pallas_call x1, Pallas kernels, per_device(): pl.pallas_call(whole_kernel, out_shape=(jax.ShapeDtypeStruct((12, HD), BF...  95 us
    unnamed x2, local copies, waits for them, and re-layouts  2.55 us

profile of v1, /device:TPU:14, one launch (start us, length us, event | category | flops | bytes accessed | tf_op | source)
XLA Modules:
  0.0 98.2 jit_solution(1654273471709195601)
XLA Ops:
  0.6 95.0 %shard_map.68 = (bf16[12,128]{1,0:T(8,128)(2,1)}, bf16[18,128]{1,0:T(8,128)(2,1)}) custom-call(bf16[1,24,128,128]{3,2,1,0:T(8,128)(2,1)} %q_hbm.1, bf16[1,24,128,128]{3,2,1,0:T(8,128)(2,1)} %k_hbm.1, bf16[1,24,128,128]{3,2,1,0:T(8,128)(2,1)} %v_hbm.1, bf16[1,24,128,128]{3,2,1,0:T(8,128)(2,1)} %u_hbm.1, bf16[1,512,1536]{2,1,0:T(8,128)(2,1)} %acts_hbm.1), custom_call_target="tpu_custom_call" | custom-call | flops 4000000000 | bytes 5000000 | tf_op jit(solution)/shard_map/pallas_call | solution.py:390
  95.7 1.3 %copy.9 = bf16[12,128]{1,0:T(8,128)(2,1)} copy(bf16[12,128]{1,0:T(8,128)(2,1)} %get-tuple-element.4) | data formatting | bytes 6144
  96.9 1.3 %copy.10 = bf16[18,128]{1,0:T(8,128)(2,1)} copy(bf16[18,128]{1,0:T(8,128)(2,1)} %get-tuple-element.5) | data formatting | bytes 9216

commit v2 on v1

--- a/solution.py
+++ b/solution.py
@@ -12,6 +12,9 @@
 GROUP = XN * YN * ZN
 HD = 128
 LEN = 512
+HALF = HD // 2
+FOLDED = HALF + 8
+PIECES = FOLDED // 8
 OWN = 6
 QUERIES = 256
 PANEL = 16
@@ -52,6 +55,36 @@
     yield 0, sum(dot(g, g, 1, 1) for g in query_grad)
 
 
+def fold(block):
+    row = lax.broadcasted_iota(jnp.int32, (HALF, HD), 0)
+    lane = lax.broadcasted_iota(jnp.int32, (HALF, HD), 1)
+    top, bottom = block[:HALF], pltpu.roll(block[HALF:], HALF, 1)
+    mixed = jnp.where((lane < HALF) & (lane <= row), bottom, top)
+    diagonal = jnp.sum(jnp.where(lane == row, top, 0.0), axis=0, keepdims=True)
+    return mixed, jnp.broadcast_to(diagonal, (8, HD))
+
+
+def unfold(mixed, diagonal):
+    row = lax.broadcasted_iota(jnp.int32, (HALF, HD), 0)
+    lane = lax.broadcasted_iota(jnp.int32, (HALF, HD), 1)
+    turned = pltpu.roll(mixed, HALF, 1)
+    upper = jnp.concatenate(
+        [
+            jnp.where((lane < HALF) & (lane <= row), 0.0, mixed),
+            jnp.where((lane >= HALF) & (lane - HALF < row), turned, 0.0),
+        ],
+        0,
+    )
+    middle = jnp.concatenate(
+        [
+            jnp.where(lane == row, diagonal, 0.0),
+            jnp.where(lane - HALF == row, turned, 0.0),
+        ],
+        0,
+    )
+    return upper + upper.T, middle
+
+
 def invert_in_place(a_ref):
     lane = lax.broadcasted_iota(jnp.int32, (8, HD), 1)
     row = lax.broadcasted_iota(jnp.int32, (PANEL, HD), 0).reshape(PANEL // 8, 8, HD)
@@ -150,6 +183,11 @@
 
     stage_slots = ((0, 3), (3, 3), (6, 1), (7, 1))
 
+    def store_gram(owner, slot, value):
+        mixed, diagonal = fold(value)
+        gram[owner, slot, pl.ds(0, HALF)] = mixed
+        gram[owner, slot, pl.ds(HALF, 8)] = diagonal
+
     def act_copy(r):
         to = (x + r) % XN
         return copy(
@@ -177,14 +215,15 @@
         wait_bytes(buf.at[t], buf_recv.at[t])
         for p, block_gram in head_grams([buf[t, i] for i in range(4)]):
             unused, owner, slot, unused = grad_place(t, p)
-            gram[owner, slot] = block_gram
+            store_gram(owner, slot, block_gram)
             owner, send = grad_copy(t, p)
             pl.when(owner != x)(send.start)
 
-    def z_piece(stage, to):
-        first, count = stage_slots[stage]
-        src = x_sum.at[pl.ds(first, count), pl.ds(pl.multiple_of(to * 8, 8), 8), :]
-        return src, z_in.at[z, pl.ds(first, count)]
+    def piece_owner(j):
+        return (ZN * j) // PIECES
+
+    my_piece = (PIECES * z + PIECES - 1) // ZN
+    holder = piece_owner(my_piece) == z
 
     def sum_x(stage):
         first, count = stage_slots[stage]
@@ -192,41 +231,40 @@
         wait_bytes(x_in.at[:, slots], x_recv.at[stage])
         for s in range(first, first + count):
             x_sum[s] = (gram[x, s] + x_in[0, s]) + (x_in[1, s] + x_in[2, s])
-
-        def send(to, carry):
-            src, dst = z_piece(stage, to)
-
-            @pl.when(to != z)
+        for j in range(PIECES):
+            to = piece_owner(j)
+            src, dst = x_sum.at[slots, pl.ds(8 * j, 8), :], z_in.at[z, slots]
+
+            @pl.when(z != to)
             def _():
                 copy(
                     src, dst, z_send.at[stage], z_recv.at[stage], place(to, y, x, head)
                 ).start()
 
-            @pl.when(to == z)
+            @pl.when(z == to)
             def _():
                 pltpu.make_async_copy(src, dst, z_recv.at[stage]).start()
 
-            return carry
-
-        lax.fori_loop(0, ZN, send, 0)
-
     def sum_z(stage):
         first, count = stage_slots[stage]
-        wait_bytes(z_in.at[:, pl.ds(first, count)], z_recv.at[stage])
-        for s in range(first, first + count):
-            z_sum[s] = jnp.sum(z_in[:, s], axis=0)
-            dst = parts.at[y, pl.ds(pl.multiple_of(z * 8, 8), 8), :]
-            mine = (z == 2 * s) & (y == 0)
-
-            @pl.when(jnp.logical_not(mine))
-            def _():
-                copy(
-                    z_sum.at[s], dst, g_send.at[s], g_recv, place(2 * s, 0, x, head)
-                ).start()
-
-            @pl.when(mine)
-            def _():
-                pltpu.make_async_copy(z_sum.at[s], dst, g_recv).start()
+
+        @pl.when(holder)
+        def _():
+            wait_bytes(z_in.at[:, pl.ds(first, count)], z_recv.at[stage])
+            for s in range(first, first + count):
+                z_sum[s] = jnp.sum(z_in[:, s], axis=0)
+                dst = parts.at[y, pl.ds(pl.multiple_of(my_piece * 8, 8), 8), :]
+                mine = (z == 2 * s) & (y == 0)
+
+                @pl.when(jnp.logical_not(mine))
+                def _():
+                    copy(
+                        z_sum.at[s], dst, g_send.at[s], g_recv, place(2 * s, 0, x, head)
+                    ).start()
+
+                @pl.when(mine)
+                def _():
+                    pltpu.make_async_copy(z_sum.at[s], dst, g_recv).start()
 
     late = x < 3
 
@@ -244,11 +282,19 @@
             act_copy(r).wait_send()
         for stage, (first, count) in enumerate(stage_slots):
             def drain_stage():
-                wait_bytes(z_in.at[pl.ds(0, ZN - 1), pl.ds(first, count)], z_send.at[stage])
-                for s in range(first, first + count):
-                    @pl.when(jnp.logical_not((z == 2 * s) & (y == 0)))
-                    def _():
-                        wait_bytes(z_sum.at[s], g_send.at[s])
+                @pl.when(holder)
+                def _():
+                    wait_bytes(
+                        z_in.at[pl.ds(0, PIECES - 1), pl.ds(first, count)], z_send.at[stage]
+                    )
+                    for s in range(first, first + count):
+                        @pl.when(jnp.logical_not((z == 2 * s) & (y == 0)))
+                        def _():
+                            wait_bytes(z_sum.at[s], g_send.at[s])
+
+                @pl.when(jnp.logical_not(holder))
+                def _():
+                    wait_bytes(z_in.at[pl.ds(0, PIECES), pl.ds(first, count)], z_send.at[stage])
 
             drain_stage() if stage < 2 else pl.when(late)(drain_stage)
 
@@ -269,17 +315,13 @@
 
     lax.fori_loop(1, GROUP, greet, 0)
     pl.semaphore_wait(barrier, GROUP - 1 + 3)
-
-    def start(t, carry):
+    for t in range(3):
         start_head(t)
-        return carry
-
-    lax.fori_loop(0, OWN, start, 0)
     load.wait()
 
     def act_gram(b, carry):
         item = acts[:, pl.ds(pl.multiple_of(b * HD, HD), HD)]
-        gram[b // 3, b % 3] = dot(item, item, 0, 0)
+        store_gram(b // 3, b % 3, dot(item, item, 0, 0))
         return carry
 
     lax.fori_loop(0, 12, act_gram, 0)
@@ -287,6 +329,10 @@
         act_copy(r).start()
 
     def step(t, carry):
+        @pl.when(t + 2 < OWN)
+        def _():
+            start_head(t + 2)
+
         @pl.when(t == 3)
         def _():
             sum_x(0)
@@ -325,8 +371,9 @@
             jnp.int32, (HD, HD), 1
         )
         total = parts[0] + parts[1]
-        trace = jnp.sum(jnp.where(eye, total, 0.0), axis=(0, 1), keepdims=True)
-        block[...] = total / (trace / HD + 1e-06) + jnp.where(eye, DAMPING, 0.0)
+        outside, middle = unfold(total[:HALF], total[HALF : HALF + 1])
+        trace = jnp.sum(middle, axis=(0, 1), keepdims=True)
+        block[...] = (outside + middle) / (trace / HD + 1e-06) + jnp.where(eye, DAMPING, 0.0)
         invert_in_place(block)
 
 
@@ -398,12 +445,12 @@
         scratch_shapes=[
             pltpu.VMEM((LEN, 12 * HD), BF16),
             pltpu.VMEM((OWN, 4, LEN, HD), BF16),
-            pltpu.VMEM((XN, SLOTS, HD, HD), F32),
-            pltpu.VMEM((XN - 1, SLOTS, HD, HD), F32),
-            pltpu.VMEM((SLOTS, HD, HD), F32),
+            pltpu.VMEM((XN, SLOTS, FOLDED, HD), F32),
+            pltpu.VMEM((XN - 1, SLOTS, FOLDED, HD), F32),
+            pltpu.VMEM((SLOTS, FOLDED, HD), F32),
             pltpu.VMEM((ZN, SLOTS, 8, HD), F32),
             pltpu.VMEM((SLOTS, 8, HD), F32),
-            pltpu.VMEM((YN, HD, HD), F32),
+            pltpu.VMEM((YN, FOLDED, HD), F32),
             pltpu.VMEM((HD, HD), F32),
             pltpu.VMEM((16, HD), F32),
             pltpu.VMEM((24, HD), F32),

time: 98.4 us -> 93.9 us (0.954)
  Pallas kernels: 95 us -> 90.5 us
    pallas_call x1, Pallas kernels: 95 us -> 90.5 us  [per_device(): pl.pallas_call(whole_kernel, out_shape=(jax.ShapeDtypeStruct((12, HD), BF...]
where the time goes in v2:
time: 93.9 us; the launch traced here: 93.6 us
  Pallas kernels  90.5 us (96%)
  local copies, waits for them, and re-layouts  2.55 us (3%)
    pallas_call x1, Pallas kernels, per_device(): pl.pallas_call(whole_kernel, out_shape=(jax.ShapeDtypeStruct((12, HD), BF...  90.5 us
    unnamed x2, local copies, waits for them, and re-layouts  2.55 us

profile of v2, /device:TPU:14, one launch (start us, length us, event | category | flops | bytes accessed | tf_op | source)
XLA Modules:
  0.0 93.6 jit_solution(14663057807002043417)
XLA Ops:
  0.6 90.5 %shard_map.68 = (bf16[12,128]{1,0:T(8,128)(2,1)}, bf16[18,128]{1,0:T(8,128)(2,1)}) custom-call(bf16[1,24,128,128]{3,2,1,0:T(8,128)(2,1)} %q_hbm.1, bf16[1,24,128,128]{3,2,1,0:T(8,128)(2,1)} %k_hbm.1, bf16[1,24,128,128]{3,2,1,0:T(8,128)(2,1)} %v_hbm.1, bf16[1,24,128,128]{3,2,1,0:T(8,128)(2,1)} %u_hbm.1, bf16[1,512,1536]{2,1,0:T(8,128)(2,1)} %acts_hbm.1), custom_call_target="tpu_custom_call" | custom-call | flops 4000000000 | bytes 5000000 | tf_op jit(solution)/shard_map/pallas_call | solution.py:437
  91.1 1.3 %copy.9 = bf16[12,128]{1,0:T(8,128)(2,1)} copy(bf16[12,128]{1,0:T(8,128)(2,1)} %get-tuple-element.4) | data formatting | bytes 6144
  92.4 1.3 %copy.10 = bf16[18,128]{1,0:T(8,128)(2,1)} copy(bf16[18,128]{1,0:T(8,128)(2,1)} %get-tuple-element.5) | data formatting | bytes 9216

commit v3 on v2

--- a/solution.py
+++ b/solution.py
@@ -16,7 +16,7 @@
 FOLDED = HALF + 8
 PIECES = FOLDED // 8
 OWN = 6
-QUERIES = 256
+KEYS = 32
 PANEL = 16
 SLOTS = 8
 SCALE = 1.0 / math.sqrt(HD)
@@ -30,29 +30,40 @@
     return lax.dot_general(a, b, (((a_dim,), (b_dim,)), ((), ())), preferred_element_type=F32)
 
 
-def head_grams(rows):
+def head_grams(rows, scores, probs_grad, probs_half, score_grad):
     q, k, v, u = rows[0], rows[1], rows[2], rows[3]
-    blocks = range(0, LEN, QUERIES)
-    probs, probs_half = [], []
-    for i in blocks:
-        scores = dot(k, q[i : i + QUERIES], 1, 1)
-        top = jnp.max(scores, axis=0, keepdims=True)
-        weights = jnp.exp2((scores - top) * (SCALE * LOG2E))
-        probs.append(weights * (1.0 / jnp.sum(weights, axis=0, keepdims=True)))
-        probs_half.append(probs[-1].astype(BF16))
-    probs_grad = [dot(v, u[i : i + QUERIES], 1, 1) for i in blocks]
-    score_grad = []
-    for full, half, grad in zip(probs, probs_half, probs_grad):
-        row_delta = jnp.sum(half.astype(F32) * grad, axis=0, keepdims=True)
-        score_grad.append((full * (grad - row_delta)).astype(BF16))
-    value_grad = sum(dot(p, u[i : i + QUERIES], 1, 0) for p, i in zip(probs_half, blocks))
-    value_grad = value_grad.astype(BF16)
+    pieces = [pl.ds(i, KEYS) for i in range(0, LEN, KEYS)]
+
+    def rows_of_eight(piece):
+        return piece.reshape(KEYS // 8, 8, LEN)
+
+    scores[...] = dot(k, q, 1, 1)
+    probs_grad[...] = dot(v, u, 1, 1)
+    top = jnp.full((8, LEN), -jnp.inf, F32)
+    for at in pieces:
+        top = jnp.maximum(top, jnp.max(rows_of_eight(scores[at, :]), axis=0))
+    top = jnp.max(top, axis=0, keepdims=True)
+    total = jnp.zeros((8, LEN), F32)
+    for at in pieces:
+        weights = jnp.exp2((scores[at, :] - top) * (SCALE * LOG2E))
+        scores[at, :] = weights
+        total += jnp.sum(rows_of_eight(weights), axis=0)
+    share = 1.0 / jnp.sum(total, axis=0, keepdims=True)
+    row_delta = jnp.zeros((8, LEN), F32)
+    for at in pieces:
+        half = (scores[at, :] * share).astype(BF16)
+        probs_half[at, :] = half
+        row_delta += jnp.sum(rows_of_eight(half.astype(F32) * probs_grad[at, :]), axis=0)
+    row_delta = jnp.sum(row_delta, axis=0, keepdims=True)
+    for at in pieces:
+        grad = scores[at, :] * share * (probs_grad[at, :] - row_delta)
+        score_grad[at, :] = grad.astype(BF16)
+    value_grad = dot(probs_half[...], u, 1, 0).astype(BF16)
     yield 2, dot(value_grad, value_grad, 0, 0)
-    key_grad = sum(dot(g, q[i : i + QUERIES], 1, 0) for g, i in zip(score_grad, blocks))
-    key_grad = (key_grad * SCALE).astype(BF16)
+    key_grad = (dot(score_grad[...], q, 1, 0) * SCALE).astype(BF16)
     yield 1, dot(key_grad, key_grad, 0, 0)
-    query_grad = [(dot(k, g, 0, 0) * SCALE).astype(BF16) for g in score_grad]
-    yield 0, sum(dot(g, g, 1, 1) for g in query_grad)
+    query_grad = (dot(k, score_grad[...], 0, 0) * SCALE).astype(BF16)
+    yield 0, dot(query_grad, query_grad, 1, 1)
 
 
 def fold(block):
@@ -137,6 +148,7 @@
     acts, buf, gram, x_in, x_sum, z_in, z_sum, parts, block, act_win, grad_win,
     acts_sem, buf_recv, core_send, far_send,
     xa_send, xg_send, x_recv, z_send, z_recv, g_send, g_recv, w_send, act_recv, grad_recv,
+    *work,
 ):
     tensors = (q_hbm, k_hbm, v_hbm, u_hbm)
     dp = lax.axis_index("dp")
@@ -213,7 +225,7 @@
 
     def compute_head(t):
         wait_bytes(buf.at[t], buf_recv.at[t])
-        for p, block_gram in head_grams([buf[t, i] for i in range(4)]):
+        for p, block_gram in head_grams([buf[t, i] for i in range(4)], *work):
             unused, owner, slot, unused = grad_place(t, p)
             store_gram(owner, slot, block_gram)
             owner, send = grad_copy(t, p)
@@ -457,6 +469,10 @@
             dma, dma((OWN,)), dma((OWN,)), dma((OWN,)),
             dma((3,)), dma((18,)), dma((4,)), dma((4,)), dma((4,)), dma((SLOTS,)), dma,
             dma((3, 12)), dma((2,)), dma((3,)),
+            pltpu.VMEM((LEN, LEN), F32),
+            pltpu.VMEM((LEN, LEN), F32),
+            pltpu.VMEM((LEN, LEN), BF16),
+            pltpu.VMEM((LEN, LEN), BF16),
         ],
         compiler_params=pltpu.CompilerParams(
             collective_id=0, has_side_effects=True, vmem_limit_bytes=62 * 1024 * 1024

time: 93.9 us -> 94.2 us (level)
  no operation moved by 1% of the time
where the time goes in v3:
time: 94.2 us; the launch traced here: 94 us
  Pallas kernels  90.8 us (96%)
  local copies, waits for them, and re-layouts  2.55 us (3%)
    pallas_call x1, Pallas kernels, per_device(): pl.pallas_call(whole_kernel, out_shape=(jax.ShapeDtypeStruct((12, HD), BF...  90.8 us
    unnamed x2, local copies, waits for them, and re-layouts  2.55 us

profile of v3, /device:TPU:14, one launch (start us, length us, event | category | flops | bytes accessed | tf_op | source)
XLA Modules:
  0.0 94.0 jit_solution(16949890105722220562)
XLA Ops:
  0.6 90.8 %shard_map.68 = (bf16[12,128]{1,0:T(8,128)(2,1)}, bf16[18,128]{1,0:T(8,128)(2,1)}) custom-call(bf16[1,24,128,128]{3,2,1,0:T(8,128)(2,1)} %q_hbm.1, bf16[1,24,128,128]{3,2,1,0:T(8,128)(2,1)} %k_hbm.1, bf16[1,24,128,128]{3,2,1,0:T(8,128)(2,1)} %v_hbm.1, bf16[1,24,128,128]{3,2,1,0:T(8,128)(2,1)} %u_hbm.1, bf16[1,512,1536]{2,1,0:T(8,128)(2,1)} %acts_hbm.1), custom_call_target="tpu_custom_call" | custom-call | flops 4000000000 | bytes 5000000 | tf_op jit(solution)/shard_map/pallas_call | solution.py:449
  91.5 1.3 %copy.9 = bf16[12,128]{1,0:T(8,128)(2,1)} copy(bf16[12,128]{1,0:T(8,128)(2,1)} %get-tuple-element.4) | data formatting | bytes 6144
  92.7 1.3 %copy.10 = bf16[18,128]{1,0:T(8,128)(2,1)} copy(bf16[18,128]{1,0:T(8,128)(2,1)} %get-tuple-element.5) | data formatting | bytes 9216

commit v4 on v2

--- a/solution.py
+++ b/solution.py
@@ -17,7 +17,7 @@
 PIECES = FOLDED // 8
 OWN = 6
 QUERIES = 256
-PANEL = 16
+PANEL = 32
 SLOTS = 8
 SCALE = 1.0 / math.sqrt(HD)
 LOG2E = 1.4426950408889634
@@ -459,7 +459,7 @@
             dma((3, 12)), dma((2,)), dma((3,)),
         ],
         compiler_params=pltpu.CompilerParams(
-            collective_id=0, has_side_effects=True, vmem_limit_bytes=62 * 1024 * 1024
+            collective_id=0, has_side_effects=True, vmem_limit_bytes=54784 * 1024
         ),
         cost_estimate=pl.CostEstimate(
             flops=4_000_000_000, bytes_accessed=5_000_000, transcendentals=1_600_000

time: 93.9 us -> 91.7 us (0.977)
  local copies, waits for them, and re-layouts: 2.55 us -> 1.19 us
    unnamed x2, local copies, waits for them, and re-layouts: 2.55 us -> 1.19 us
where the time goes in v4:
time: 91.7 us; the launch traced here: 91.6 us
  Pallas kernels  89.8 us (98%)
  local copies, waits for them, and re-layouts  1.19 us (1%)
    pallas_call x1, Pallas kernels, per_device(): pl.pallas_call(whole_kernel, out_shape=(jax.ShapeDtypeStruct((12, HD), BF...  89.8 us

profile of v4, /device:TPU:14, one launch (start us, length us, event | category | flops | bytes accessed | tf_op | source)
XLA Modules:
  0.0 91.6 jit_solution(14645848404024372341)
XLA Ops:
  0.6 89.8 %shard_map.68 = (bf16[12,128]{1,0:T(8,128)(2,1)S(1)}, bf16[18,128]{1,0:T(8,128)(2,1)S(1)}) custom-call(bf16[1,24,128,128]{3,2,1,0:T(8,128)(2,1)} %q_hbm.1, bf16[1,24,128,128]{3,2,1,0:T(8,128)(2,1)} %k_hbm.1, bf16[1,24,128,128]{3,2,1,0:T(8,128)(2,1)} %v_hbm.1, bf16[1,24,128,128]{3,2,1,0:T(8,128)(2,1)} %u_hbm.1, bf16[1,512,1536]{2,1,0:T(8,128)(2,1)} %acts_hbm.1), custom_call_target="tpu_custom_call" | custom-call | flops 4000000000 | bytes 5000000 | tf_op jit(solution)/shard_map/pallas_call | solution.py:437
  90.4 0.6 copy.9
  91.0 0.6 copy.10

commit v5 on v4

--- a/solution.py
+++ b/solution.py
@@ -17,7 +17,7 @@
 PIECES = FOLDED // 8
 OWN = 6
 QUERIES = 256
-PANEL = 32
+PANEL = 64
 SLOTS = 8
 SCALE = 1.0 / math.sqrt(HD)
 LOG2E = 1.4426950408889634
@@ -30,8 +30,8 @@
     return lax.dot_general(a, b, (((a_dim,), (b_dim,)), ((), ())), preferred_element_type=F32)
 
 
-def head_grams(rows):
-    q, k, v, u = rows[0], rows[1], rows[2], rows[3]
+def head_grams(first_rows, last_rows):
+    q, k = first_rows()
     blocks = range(0, LEN, QUERIES)
     probs, probs_half = [], []
     for i in blocks:
@@ -40,6 +40,7 @@
         weights = jnp.exp2((scores - top) * (SCALE * LOG2E))
         probs.append(weights * (1.0 / jnp.sum(weights, axis=0, keepdims=True)))
         probs_half.append(probs[-1].astype(BF16))
+    v, u = last_rows()
     probs_grad = [dot(v, u[i : i + QUERIES], 1, 1) for i in blocks]
     score_grad = []
     for full, half, grad in zip(probs, probs_half, probs_grad):
@@ -135,7 +136,7 @@
 def whole_kernel(
     q_hbm, k_hbm, v_hbm, u_hbm, acts_hbm, act_out, grad_out,
     acts, buf, gram, x_in, x_sum, z_in, z_sum, parts, block, act_win, grad_win,
-    acts_sem, buf_recv, core_send, far_send,
+    acts_sem, buf_recv, far_send,
     xa_send, xg_send, x_recv, z_send, z_recv, g_send, g_recv, w_send, act_recv, grad_recv,
 ):
     tensors = (q_hbm, k_hbm, v_hbm, u_hbm)
@@ -163,22 +164,16 @@
         return pl.ds(pl.multiple_of(source * HD, HD), HD)
 
     def start_head(t):
+        other = half * 2 + 1 - core
         for i in range(4):
-            for far in range(2):
-                to = (1 - half) * 2 + far
+            for to in ((1 - half) * 2, (1 - half) * 2 + 1, other):
                 copy(
                     tensors[i].at[0, to * OWN + t], buf.at[t, i, rows_of(head), :],
-                    far_send.at[t], buf_recv.at[t], place(z, y, x, to),
+                    far_send.at[t], buf_recv.at[t, i // 2], place(z, y, x, to),
                 ).start()
-        other = half * 2 + 1 - core
-        for i in range(4):
-            copy(
-                tensors[i].at[0, other * OWN + t], buf.at[t, i, rows_of(head), :],
-                core_send.at[t], buf_recv.at[t], place(z, y, x, other),
-            ).start()
             pltpu.make_async_copy(
                 tensors[i].at[0, head * OWN + t], buf.at[t, i, rows_of(head), :],
-                buf_recv.at[t],
+                buf_recv.at[t, i // 2],
             ).start()
 
     stage_slots = ((0, 3), (3, 3), (6, 1), (7, 1))
@@ -212,8 +207,11 @@
         )
 
     def compute_head(t):
-        wait_bytes(buf.at[t], buf_recv.at[t])
-        for p, block_gram in head_grams([buf[t, i] for i in range(4)]):
+        def rows(pair):
+            wait_bytes(buf.at[t, pl.ds(2 * pair, 2)], buf_recv.at[t, pair])
+            return buf[t, 2 * pair], buf[t, 2 * pair + 1]
+
+        for p, block_gram in head_grams(lambda: rows(0), lambda: rows(1)):
             unused, owner, slot, unused = grad_place(t, p)
             store_gram(owner, slot, block_gram)
             owner, send = grad_copy(t, p)
@@ -270,8 +268,7 @@
 
     def drain():
         def sent(t, carry):
-            wait_bytes(buf.at[t, :, pl.ds(0, 2 * HD), :], far_send.at[t])
-            wait_bytes(buf.at[t, :, pl.ds(0, HD), :], core_send.at[t])
+            wait_bytes(buf.at[t, :, pl.ds(0, 3 * HD), :], far_send.at[t])
             for p in range(3):
                 owner, send = grad_copy(t, p)
                 pl.when(owner != x)(send.wait_send)
@@ -454,7 +451,7 @@
             pltpu.VMEM((HD, HD), F32),
             pltpu.VMEM((16, HD), F32),
             pltpu.VMEM((24, HD), F32),
-            dma, dma((OWN,)), dma((OWN,)), dma((OWN,)),
+            dma, dma((OWN, 2)), dma((OWN,)),
             dma((3,)), dma((18,)), dma((4,)), dma((4,)), dma((4,)), dma((SLOTS,)), dma,
             dma((3, 12)), dma((2,)), dma((3,)),
         ],

time: 91.7 us -> 91 us (level)
  no operation moved by 1% of the time
where the time goes in v5:
time: 91 us; the launch traced here: 90.9 us
  Pallas kernels  89.1 us (98%)
  local copies, waits for them, and re-layouts  1.19 us (1%)
    pallas_call x1, Pallas kernels, per_device(): pl.pallas_call(whole_kernel, out_shape=(jax.ShapeDtypeStruct((12, HD), BF...  89.1 us

profile of v5, /device:TPU:14, one launch (start us, length us, event | category | flops | bytes accessed | tf_op | source)
XLA Modules:
  0.0 90.9 jit_solution(6832875954705003241)
XLA Ops:
  0.6 89.1 %shard_map.68 = (bf16[12,128]{1,0:T(8,128)(2,1)S(1)}, bf16[18,128]{1,0:T(8,128)(2,1)S(1)}) custom-call(bf16[1,24,128,128]{3,2,1,0:T(8,128)(2,1)} %q_hbm.1, bf16[1,24,128,128]{3,2,1,0:T(8,128)(2,1)} %k_hbm.1, bf16[1,24,128,128]{3,2,1,0:T(8,128)(2,1)} %v_hbm.1, bf16[1,24,128,128]{3,2,1,0:T(8,128)(2,1)} %u_hbm.1, bf16[1,512,1536]{2,1,0:T(8,128)(2,1)} %acts_hbm.1), custom_call_target="tpu_custom_call" | custom-call | flops 4000000000 | bytes 5000000 | tf_op jit(solution)/shard_map/pallas_call | solution.py:434
  89.7 0.6 copy.9
  90.3 0.6 copy.10

commit v6 on v5

--- a/solution.py
+++ b/solution.py
@@ -138,8 +138,8 @@
     acts, buf, gram, x_in, x_sum, z_in, z_sum, parts, block, act_win, grad_win,
     acts_sem, buf_recv, far_send,
     xa_send, xg_send, x_recv, z_send, z_recv, g_send, g_recv, w_send, act_recv, grad_recv,
+    staged, staged_sem,
 ):
-    tensors = (q_hbm, k_hbm, v_hbm, u_hbm)
     dp = lax.axis_index("dp")
     head = lax.axis_index("head")
     x = dp % XN
@@ -168,11 +168,11 @@
         for i in range(4):
             for to in ((1 - half) * 2, (1 - half) * 2 + 1, other):
                 copy(
-                    tensors[i].at[0, to * OWN + t], buf.at[t, i, rows_of(head), :],
+                    staged.at[i, to * OWN + t], buf.at[t, i, rows_of(head), :],
                     far_send.at[t], buf_recv.at[t, i // 2], place(z, y, x, to),
                 ).start()
             pltpu.make_async_copy(
-                tensors[i].at[0, head * OWN + t], buf.at[t, i, rows_of(head), :],
+                staged.at[i, head * OWN + t], buf.at[t, i, rows_of(head), :],
                 buf_recv.at[t, i // 2],
             ).start()
 
@@ -296,6 +296,12 @@
             drain_stage() if stage < 2 else pl.when(late)(drain_stage)
 
     load = pltpu.make_async_copy(acts_hbm.at[0], acts, acts_sem)
+    stage = [
+        pltpu.make_async_copy(ref.at[0], staged.at[i], staged_sem.at[i])
+        for i, ref in enumerate((q_hbm, k_hbm, v_hbm, u_hbm))
+    ]
+    for item in stage:
+        item.start()
     load.start()
 
     barrier = pltpu.get_barrier_semaphore()
@@ -311,6 +317,8 @@
         return carry
 
     lax.fori_loop(1, GROUP, greet, 0)
+    for item in stage:
+        item.wait()
     pl.semaphore_wait(barrier, GROUP - 1 + 3)
     for t in range(3):
         start_head(t)
@@ -454,6 +462,7 @@
             dma, dma((OWN, 2)), dma((OWN,)),
             dma((3,)), dma((18,)), dma((4,)), dma((4,)), dma((4,)), dma((SLOTS,)), dma,
             dma((3, 12)), dma((2,)), dma((3,)),
+            pltpu.VMEM((4, 4 * OWN, HD, HD), BF16), dma((4,)),
         ],
         compiler_params=pltpu.CompilerParams(
             collective_id=0, has_side_effects=True, vmem_limit_bytes=54784 * 1024

time: 91 us -> 90.2 us (level)
  no operation moved by 1% of the time
where the time goes in v6:
time: 90.2 us; the launch traced here: 90.1 us
  Pallas kernels  88.3 us (98%)
  local copies, waits for them, and re-layouts  1.19 us (1%)
    pallas_call x1, Pallas kernels, per_device(): pl.pallas_call(whole_kernel, out_shape=(jax.ShapeDtypeStruct((12, HD), BF...  88.3 us

profile of v6, /device:TPU:14, one launch (start us, length us, event | category | flops | bytes accessed | tf_op | source)
XLA Modules:
  0.0 90.1 jit_solution(18369037135298806654)
XLA Ops:
  0.6 88.3 %shard_map.68 = (bf16[12,128]{1,0:T(8,128)(2,1)S(1)}, bf16[18,128]{1,0:T(8,128)(2,1)S(1)}) custom-call(bf16[1,24,128,128]{3,2,1,0:T(8,128)(2,1)} %q_hbm.1, bf16[1,24,128,128]{3,2,1,0:T(8,128)(2,1)} %k_hbm.1, bf16[1,24,128,128]{3,2,1,0:T(8,128)(2,1)} %v_hbm.1, bf16[1,24,128,128]{3,2,1,0:T(8,128)(2,1)} %u_hbm.1, bf16[1,512,1536]{2,1,0:T(8,128)(2,1)} %acts_hbm.1), custom_call_target="tpu_custom_call" | custom-call | flops 4000000000 | bytes 5000000 | tf_op jit(solution)/shard_map/pallas_call | solution.py:442
  88.9 0.6 copy.9
  89.5 0.6 copy.10
